TPU v7x, 256 devices: a whole 4x4x8 slice. The times are simulated.
256 devices in a mesh: pipe: 8 (over x, core), graph: 32 (over y, z).
Axes of the slice: x: 4, y: 4, z: 8, core: 2. Of those that a mesh axis runs over, the one named last changes fastest.
Arguments:
- features: bfloat16 [4, 8192, 1024], P(None, 'graph'), may hold values from -6 to 6
- weights: bfloat16 [8, 1024, 1024], P('pipe'), may hold values from -0.1875 to 0.1875
- gains: float32 [8, 1024], P('pipe'), may hold values from 0.5 to 1.5
- tiles: bfloat16 [4, 384, 128, 128], P(None, 'graph'), may hold values from 0 to 0.16764323, as said below
- tile_coords: int32 [4, 384, 2], P(None, 'graph'), may hold values from 0 to 3, as said below
- send_ids: int32 [4, 32, 2, 1], replicated, may hold values from 0 to 1
Outputs:
- activations: bfloat16 [8, 4, 8192, 1024], P('pipe', None, 'graph')
Inputs may be any that keep to these rules, and one draw needn't show every extreme that they name: `tile_coords`: each row is (destination block, source slot): slots below 2 are the partition's own blocks, the next 1 come from the partition before, the last 1 from the partition after; in every micro-batch and partition every slot and every destination block is named by some tile. `tiles`: nonnegative adjacency weights.
All inputs are finite; a program needn't handle non-finite values.
Results may differ from a plain program's by a relative error of at most 0.0085.
Values may be sent and summed in bfloat16 or wider, within the bound.
A program may use at most 64 MiB of HBM per device.

v0:
```python
import jax
import jax.numpy as jnp
from jax import lax
from jax.sharding import PartitionSpec as P


def with_halo(block, sides, width):
    for axis, dim in sides:
        count = lax.axis_size(axis)
        forward = [(i, i + 1) for i in range(count - 1)]
        forward.append((count - 1, 0))
        backward = [(target, source) for source, target in forward]
        low = lax.ppermute(
            lax.slice_in_dim(block, block.shape[dim] - width, None, axis=dim), axis, forward
        )
        high = lax.ppermute(lax.slice_in_dim(block, 0, width, axis=dim), axis, backward)
        block = jnp.concatenate([low, block, high], axis=dim)
    return block


def from_behind(value, axis, steps):
    count = lax.axis_size(axis)
    first, last = (max(0, -steps), min(count, count - steps))
    return lax.ppermute(value, axis, [(source, source + steps) for source in range(first, last)])


def part_layer(blocked, from_left, from_right, tile, coords, weight, gain):
    nblocks = blocked.shape[0]
    edge = blocked.shape[1]
    width = blocked.shape[2]
    count = tile.shape[0]
    sources = jnp.concatenate([blocked, from_left, from_right], axis=0)
    slots = sources.shape[0]
    dest_hot = (coords[:, 0][:, None] == jnp.arange(nblocks, dtype=jnp.int32)[None, :]).astype(
        jnp.float32
    )
    slot_hot = (coords[:, 1][:, None] == jnp.arange(slots, dtype=jnp.int32)[None, :]).astype(
        jnp.float32
    )
    pairing = (dest_hot[:, :, None] * slot_hot[:, None, :]).reshape(count, nblocks * slots)
    flat_tiles = tile.astype(jnp.float32).reshape(count, edge * edge)
    table = jnp.dot(pairing.T, flat_tiles, precision=lax.Precision.HIGHEST)
    table = table.reshape(nblocks, slots, edge, edge)
    table = (
        jnp.transpose(table, (0, 2, 1, 3))
        .reshape(nblocks * edge, slots * edge)
        .astype(jnp.bfloat16)
    )
    agg = jnp.dot(
        table, sources.reshape(slots * edge, width), preferred_element_type=jnp.float32
    ).astype(jnp.bfloat16)
    z = jnp.dot(agg, weight, preferred_element_type=jnp.float32)
    act = jnp.maximum(z, 0.0)
    scale = 1.0 / jnp.sqrt(jnp.mean(act * act, axis=-1, keepdims=True) + 1e-06)
    return (act * scale * gain[None, :]).astype(jnp.bfloat16)


def on_device(features, weights, gains, tiles, tile_coords, send_ids):
    section = lax.axis_index("pipe")
    sections = lax.axis_size("pipe")
    part_index = lax.axis_index("graph")
    partitions = lax.axis_size("graph")
    micro_count = features.shape[0]
    rows = features.shape[1]
    width = features.shape[2]
    edge = tiles.shape[-1]
    nblocks = rows // edge
    weight = weights[0]
    gain = gains[0]
    before = (part_index + partitions - 1) % partitions
    after = (part_index + 1) % partitions

    def turn(carry, step_now):
        incoming, stored = carry
        micro = step_now - section
        valid = jnp.logical_and(micro >= 0, micro < micro_count)
        index = jnp.clip(micro, 0, micro_count - 1)
        fresh = lax.dynamic_index_in_dim(features, index, 0, keepdims=False)
        current = jnp.where(section == 0, fresh, incoming)
        blocked = current.reshape(nblocks, edge, width)
        table = lax.dynamic_index_in_dim(send_ids, index, 0, keepdims=False)
        padded = with_halo(blocked, (("graph", 0),), nblocks)
        left_ids = lax.dynamic_index_in_dim(table, before, 0, keepdims=False)[0]
        right_ids = lax.dynamic_index_in_dim(table, after, 0, keepdims=False)[1]
        from_left = jnp.take(padded[:nblocks], left_ids, axis=0)
        from_right = jnp.take(padded[2 * nblocks :], right_ids, axis=0)
        tile = lax.dynamic_index_in_dim(tiles, index, 0, keepdims=False)
        coords = lax.dynamic_index_in_dim(tile_coords, index, 0, keepdims=False)
        result = part_layer(blocked, from_left, from_right, tile, coords, weight, gain)
        updated = lax.dynamic_update_index_in_dim(stored, result, index, 0)
        stored = jnp.where(valid, updated, stored)
        passed = from_behind(result, "pipe", 1)
        return ((passed, stored), None)

    start = (
        jnp.zeros((rows, width), jnp.bfloat16),
        jnp.zeros((micro_count, rows, width), jnp.bfloat16),
    )
    steps_all = jnp.arange(micro_count + sections - 1, dtype=jnp.int32)
    final, unused = lax.scan(turn, start, steps_all)
    return final[1][None]


def solution(mesh):
    placed = (
        P(None, "graph", None),
        P("pipe", None, None),
        P("pipe", None),
        P(None, "graph", None, None),
        P(None, "graph", None),
        P(),
    )
    return jax.shard_map(
        on_device,
        mesh=mesh,
        in_specs=placed,
        out_specs=P("pipe", None, "graph", None),
        check_vma=False,
    )
```

profile of v0, /device:TPU:1, one launch (start us, length us, event | category | flops | bytes accessed | tf_op | source)
XLA Modules:
  0.0 352.9 jit_solution(3831815782113618299)
XLA Ops:
  1.7 351.2 %while.16 = (s32[]{:T(128)}, bf16[256,1024]{1,0:T(8,128)(2,1)S(1)}, bf16[4,256,1024]{2,1,0:T(8,128)(2,1)}, s32[11]{0:T(128)S(1)}, s32[]{:T(128)}, /*index=5*/s32...) while((s32[]{:T(128)}, bf16[256,1024]{1,0:T(8,128)(2,1)S(1)}, ...), condition=%wide.region_2.4_spmd, body=%wide.region_0.3_spmd.sunk | while | flops 827982336 | bytes 20325992 | solution.py:100
  6.6 6.5 %collective-permute-start = (bf16[2,128,1024]{2,1,0:T(8,128)(2,1)S(1)}, bf16[2,128,1024]{2,1,0:T(8,128)(2,1)S(1)}, u32[]{:S(2)}, u32[]{:S(2)}) collective-permute-start(bf16[2,128,1024]{2,1,0:T(8,128)(2,1)S(1)} %bitcast.108), channel_id=1, source_target_pairs={{1,0},{2,1},{3,2},{4,3},{5,4},{6,5},{7,6},{8,7},{9,8},{10,9},{11,1... | collective-permute-start | bytes 1572872 | tf_op jit(solution)/shard_map/while/body/eval_jaxpr/ppermute | solution.py:16
  33.8 6.1 %collective-permute-done.2 = bf16[256,1024]{1,0:T(8,128)(2,1)S(1)} collective-permute-done((bf16[256,1024]{1,0:T(8,128)(2,1)S(1)}, bf16[256,1024]{1,0:T(8,128)(2,1)S(1)}, u32[]{:S(2)}, u32[]{:S(2)}) %collective-permute-start.2) | collective-permute-done | bytes 524320 | tf_op jit(solution)/shard_map/while/body/eval_jaxpr/ppermute | solution.py:24
  42.4 4.9 %collective-permute-start = (bf16[2,128,1024]{2,1,0:T(8,128)(2,1)S(1)}, bf16[2,128,1024]{2,1,0:T(8,128)(2,1)S(1)}, u32[]{:S(2)}, u32[]{:S(2)}) collective-permute-start(bf16[2,128,1024]{2,1,0:T(8,128)(2,1)S(1)} %bitcast.108), channel_id=1, source_target_pairs={{1,0},{2,1},{3,2},{4,3},{5,4},{6,5},{7,6},{8,7},{9,8},{10,9},{11,1... | collective-permute-start | bytes 1572872 | tf_op jit(solution)/shard_map/while/body/eval_jaxpr/ppermute | solution.py:16
  59.6 8.5 %collective-permute-start.2 = (bf16[256,1024]{1,0:T(8,128)(2,1)S(1)}, bf16[256,1024]{1,0:T(8,128)(2,1)S(1)}, u32[]{:S(2)}, u32[]{:S(2)}) collective-permute-start(bf16[256,1024]{1,0:T(8,128)(2,1)S(1)} %get-tuple-element.388), channel_id=1, source_target_pairs={{0,32},{32,64},{64,96},{96,128},{128,160},{160,192},{192,224},{1,3... | collective-permute-start | bytes 1572872 | tf_op jit(solution)/shard_map/while/body/eval_jaxpr/ppermute | solution.py:24
  68.1 6.1 %collective-permute-done.2 = bf16[256,1024]{1,0:T(8,128)(2,1)S(1)} collective-permute-done((bf16[256,1024]{1,0:T(8,128)(2,1)S(1)}, bf16[256,1024]{1,0:T(8,128)(2,1)S(1)}, u32[]{:S(2)}, u32[]{:S(2)}) %collective-permute-start.2) | collective-permute-done | bytes 524320 | tf_op jit(solution)/shard_map/while/body/eval_jaxpr/ppermute | solution.py:24
  76.7 4.9 %collective-permute-start = (bf16[2,128,1024]{2,1,0:T(8,128)(2,1)S(1)}, bf16[2,128,1024]{2,1,0:T(8,128)(2,1)S(1)}, u32[]{:S(2)}, u32[]{:S(2)}) collective-permute-start(bf16[2,128,1024]{2,1,0:T(8,128)(2,1)S(1)} %bitcast.108), channel_id=1, source_target_pairs={{1,0},{2,1},{3,2},{4,3},{5,4},{6,5},{7,6},{8,7},{9,8},{10,9},{11,1... | collective-permute-start | bytes 1572872 | tf_op jit(solution)/shard_map/while/body/eval_jaxpr/ppermute | solution.py:16
  93.8 8.2 %collective-permute-start.2 = (bf16[256,1024]{1,0:T(8,128)(2,1)S(1)}, bf16[256,1024]{1,0:T(8,128)(2,1)S(1)}, u32[]{:S(2)}, u32[]{:S(2)}) collective-permute-start(bf16[256,1024]{1,0:T(8,128)(2,1)S(1)} %get-tuple-element.388), channel_id=1, source_target_pairs={{0,32},{32,64},{64,96},{96,128},{128,160},{160,192},{192,224},{1,3... | collective-permute-start | bytes 1572872 | tf_op jit(solution)/shard_map/while/body/eval_jaxpr/ppermute | solution.py:24
  102.0 6.1 %collective-permute-done.2 = bf16[256,1024]{1,0:T(8,128)(2,1)S(1)} collective-permute-done((bf16[256,1024]{1,0:T(8,128)(2,1)S(1)}, bf16[256,1024]{1,0:T(8,128)(2,1)S(1)}, u32[]{:S(2)}, u32[]{:S(2)}) %collective-permute-start.2) | collective-permute-done | bytes 524320 | tf_op jit(solution)/shard_map/while/body/eval_jaxpr/ppermute | solution.py:24
  132.7 6.1 %collective-permute-done.2 = bf16[256,1024]{1,0:T(8,128)(2,1)S(1)} collective-permute-done((bf16[256,1024]{1,0:T(8,128)(2,1)S(1)}, bf16[256,1024]{1,0:T(8,128)(2,1)S(1)}, u32[]{:S(2)}, u32[]{:S(2)}) %collective-permute-start.2) | collective-permute-done | bytes 524320 | tf_op jit(solution)/shard_map/while/body/eval_jaxpr/ppermute | solution.py:24
  141.3 4.9 %collective-permute-start = (bf16[2,128,1024]{2,1,0:T(8,128)(2,1)S(1)}, bf16[2,128,1024]{2,1,0:T(8,128)(2,1)S(1)}, u32[]{:S(2)}, u32[]{:S(2)}) collective-permute-start(bf16[2,128,1024]{2,1,0:T(8,128)(2,1)S(1)} %bitcast.108), channel_id=1, source_target_pairs={{1,0},{2,1},{3,2},{4,3},{5,4},{6,5},{7,6},{8,7},{9,8},{10,9},{11,1... | collective-permute-start | bytes 1572872 | tf_op jit(solution)/shard_map/while/body/eval_jaxpr/ppermute | solution.py:16
  163.3 6.1 %collective-permute-done.2 = bf16[256,1024]{1,0:T(8,128)(2,1)S(1)} collective-permute-done((bf16[256,1024]{1,0:T(8,128)(2,1)S(1)}, bf16[256,1024]{1,0:T(8,128)(2,1)S(1)}, u32[]{:S(2)}, u32[]{:S(2)}) %collective-permute-start.2) | collective-permute-done | bytes 524320 | tf_op jit(solution)/shard_map/while/body/eval_jaxpr/ppermute | solution.py:24
  171.9 4.9 %collective-permute-start = (bf16[2,128,1024]{2,1,0:T(8,128)(2,1)S(1)}, bf16[2,128,1024]{2,1,0:T(8,128)(2,1)S(1)}, u32[]{:S(2)}, u32[]{:S(2)}) collective-permute-start(bf16[2,128,1024]{2,1,0:T(8,128)(2,1)S(1)} %bitcast.108), channel_id=1, source_target_pairs={{1,0},{2,1},{3,2},{4,3},{5,4},{6,5},{7,6},{8,7},{9,8},{10,9},{11,1... | collective-permute-start | bytes 1572872 | tf_op jit(solution)/shard_map/while/body/eval_jaxpr/ppermute | solution.py:16
  193.9 6.1 %collective-permute-done.2 = bf16[256,1024]{1,0:T(8,128)(2,1)S(1)} collective-permute-done((bf16[256,1024]{1,0:T(8,128)(2,1)S(1)}, bf16[256,1024]{1,0:T(8,128)(2,1)S(1)}, u32[]{:S(2)}, u32[]{:S(2)}) %collective-permute-start.2) | collective-permute-done | bytes 524320 | tf_op jit(solution)/shard_map/while/body/eval_jaxpr/ppermute | solution.py:24
  202.5 4.9 %collective-permute-start = (bf16[2,128,1024]{2,1,0:T(8,128)(2,1)S(1)}, bf16[2,128,1024]{2,1,0:T(8,128)(2,1)S(1)}, u32[]{:S(2)}, u32[]{:S(2)}) collective-permute-start(bf16[2,128,1024]{2,1,0:T(8,128)(2,1)S(1)} %bitcast.108), channel_id=1, source_target_pairs={{1,0},{2,1},{3,2},{4,3},{5,4},{6,5},{7,6},{8,7},{9,8},{10,9},{11,1... | collective-permute-start | bytes 1572872 | tf_op jit(solution)/shard_map/while/body/eval_jaxpr/ppermute | solution.py:16
  224.5 6.1 %collective-permute-done.2 = bf16[256,1024]{1,0:T(8,128)(2,1)S(1)} collective-permute-done((bf16[256,1024]{1,0:T(8,128)(2,1)S(1)}, bf16[256,1024]{1,0:T(8,128)(2,1)S(1)}, u32[]{:S(2)}, u32[]{:S(2)}) %collective-permute-start.2) | collective-permute-done | bytes 524320 | tf_op jit(solution)/shard_map/while/body/eval_jaxpr/ppermute | solution.py:24
  233.1 5.0 %collective-permute-start = (bf16[2,128,1024]{2,1,0:T(8,128)(2,1)S(1)}, bf16[2,128,1024]{2,1,0:T(8,128)(2,1)S(1)}, u32[]{:S(2)}, u32[]{:S(2)}) collective-permute-start(bf16[2,128,1024]{2,1,0:T(8,128)(2,1)S(1)} %bitcast.108), channel_id=1, source_target_pairs={{1,0},{2,1},{3,2},{4,3},{5,4},{6,5},{7,6},{8,7},{9,8},{10,9},{11,1... | collective-permute-start | bytes 1572872 | tf_op jit(solution)/shard_map/while/body/eval_jaxpr/ppermute | solution.py:16
  255.1 6.1 %collective-permute-done.2 = bf16[256,1024]{1,0:T(8,128)(2,1)S(1)} collective-permute-done((bf16[256,1024]{1,0:T(8,128)(2,1)S(1)}, bf16[256,1024]{1,0:T(8,128)(2,1)S(1)}, u32[]{:S(2)}, u32[]{:S(2)}) %collective-permute-start.2) | collective-permute-done | bytes 524320 | tf_op jit(solution)/shard_map/while/body/eval_jaxpr/ppermute | solution.py:24
  263.6 5.0 %collective-permute-start = (bf16[2,128,1024]{2,1,0:T(8,128)(2,1)S(1)}, bf16[2,128,1024]{2,1,0:T(8,128)(2,1)S(1)}, u32[]{:S(2)}, u32[]{:S(2)}) collective-permute-start(bf16[2,128,1024]{2,1,0:T(8,128)(2,1)S(1)} %bitcast.108), channel_id=1, source_target_pairs={{1,0},{2,1},{3,2},{4,3},{5,4},{6,5},{7,6},{8,7},{9,8},{10,9},{11,1... | collective-permute-start | bytes 1572872 | tf_op jit(solution)/shard_map/while/body/eval_jaxpr/ppermute | solution.py:16
  285.6 6.1 %collective-permute-done.2 = bf16[256,1024]{1,0:T(8,128)(2,1)S(1)} collective-permute-done((bf16[256,1024]{1,0:T(8,128)(2,1)S(1)}, bf16[256,1024]{1,0:T(8,128)(2,1)S(1)}, u32[]{:S(2)}, u32[]{:S(2)}) %collective-permute-start.2) | collective-permute-done | bytes 524320 | tf_op jit(solution)/shard_map/while/body/eval_jaxpr/ppermute | solution.py:24
  294.2 5.0 %collective-permute-start = (bf16[2,128,1024]{2,1,0:T(8,128)(2,1)S(1)}, bf16[2,128,1024]{2,1,0:T(8,128)(2,1)S(1)}, u32[]{:S(2)}, u32[]{:S(2)}) collective-permute-start(bf16[2,128,1024]{2,1,0:T(8,128)(2,1)S(1)} %bitcast.108), channel_id=1, source_target_pairs={{1,0},{2,1},{3,2},{4,3},{5,4},{6,5},{7,6},{8,7},{9,8},{10,9},{11,1... | collective-permute-start | bytes 1572872 | tf_op jit(solution)/shard_map/while/body/eval_jaxpr/ppermute | solution.py:16
  316.2 6.1 %collective-permute-done.2 = bf16[256,1024]{1,0:T(8,128)(2,1)S(1)} collective-permute-done((bf16[256,1024]{1,0:T(8,128)(2,1)S(1)}, bf16[256,1024]{1,0:T(8,128)(2,1)S(1)}, u32[]{:S(2)}, u32[]{:S(2)}) %collective-permute-start.2) | collective-permute-done | bytes 524320 | tf_op jit(solution)/shard_map/while/body/eval_jaxpr/ppermute | solution.py:24
  324.8 5.0 %collective-permute-start = (bf16[2,128,1024]{2,1,0:T(8,128)(2,1)S(1)}, bf16[2,128,1024]{2,1,0:T(8,128)(2,1)S(1)}, u32[]{:S(2)}, u32[]{:S(2)}) collective-permute-start(bf16[2,128,1024]{2,1,0:T(8,128)(2,1)S(1)} %bitcast.108), channel_id=1, source_target_pairs={{1,0},{2,1},{3,2},{4,3},{5,4},{6,5},{7,6},{8,7},{9,8},{10,9},{11,1... | collective-permute-start | bytes 1572872 | tf_op jit(solution)/shard_map/while/body/eval_jaxpr/ppermute | solution.py:16
  346.8 6.1 %collective-permute-done.2 = bf16[256,1024]{1,0:T(8,128)(2,1)S(1)} collective-permute-done((bf16[256,1024]{1,0:T(8,128)(2,1)S(1)}, bf16[256,1024]{1,0:T(8,128)(2,1)S(1)}, u32[]{:S(2)}, u32[]{:S(2)}) %collective-permute-start.2) | collective-permute-done | bytes 524320 | tf_op jit(solution)/shard_map/while/body/eval_jaxpr/ppermute | solution.py:24
  (224 shorter events, 170.5 us)
Async XLA Ops:
  4.0 20.6 %collective-permute-start.1 = (bf16[2,128,1024]{2,1,0:T(8,128)(2,1)S(1)}, bf16[2,128,1024]{2,1,0:T(8,128)(2,1)S(1)}, u32[]{:S(2)}, u32[]{:S(2)}) collective-permute-start(bf16[2,128,1024]{2,1,0:T(8,128)(2,1)S(1)} %bitcast.107), channel_id=1, source_target_pairs={{0,1},{1,2},{2,3},{3,4},{4,5},{5,6},{6,7},{7,8},{8,9},{9,10},{10,1... | collective-permute-start | bytes 1572872 | tf_op jit(solution)/shard_map/while/body/eval_jaxpr/ppermute | solution.py:13
  6.6 18.1 %collective-permute-start = (bf16[2,128,1024]{2,1,0:T(8,128)(2,1)S(1)}, bf16[2,128,1024]{2,1,0:T(8,128)(2,1)S(1)}, u32[]{:S(2)}, u32[]{:S(2)}) collective-permute-start(bf16[2,128,1024]{2,1,0:T(8,128)(2,1)S(1)} %bitcast.108), channel_id=1, source_target_pairs={{1,0},{2,1},{3,2},{4,3},{5,4},{6,5},{7,6},{8,7},{9,8},{10,9},{11,1... | collective-permute-start | bytes 1572872 | tf_op jit(solution)/shard_map/while/body/eval_jaxpr/ppermute | solution.py:16
  42.3 12.3 %collective-permute-start.1 = (bf16[2,128,1024]{2,1,0:T(8,128)(2,1)S(1)}, bf16[2,128,1024]{2,1,0:T(8,128)(2,1)S(1)}, u32[]{:S(2)}, u32[]{:S(2)}) collective-permute-start(bf16[2,128,1024]{2,1,0:T(8,128)(2,1)S(1)} %bitcast.107), channel_id=1, source_target_pairs={{0,1},{1,2},{2,3},{3,4},{4,5},{5,6},{6,7},{7,8},{8,9},{9,10},{10,1... | collective-permute-start | bytes 1572872 | tf_op jit(solution)/shard_map/while/body/eval_jaxpr/ppermute | solution.py:13
  42.4 12.2 %collective-permute-start = (bf16[2,128,1024]{2,1,0:T(8,128)(2,1)S(1)}, bf16[2,128,1024]{2,1,0:T(8,128)(2,1)S(1)}, u32[]{:S(2)}, u32[]{:S(2)}) collective-permute-start(bf16[2,128,1024]{2,1,0:T(8,128)(2,1)S(1)} %bitcast.108), channel_id=1, source_target_pairs={{1,0},{2,1},{3,2},{4,3},{5,4},{6,5},{7,6},{8,7},{9,8},{10,9},{11,1... | collective-permute-start | bytes 1572872 | tf_op jit(solution)/shard_map/while/body/eval_jaxpr/ppermute | solution.py:16
  59.6 14.6 %collective-permute-start.2 = (bf16[256,1024]{1,0:T(8,128)(2,1)S(1)}, bf16[256,1024]{1,0:T(8,128)(2,1)S(1)}, u32[]{:S(2)}, u32[]{:S(2)}) collective-permute-start(bf16[256,1024]{1,0:T(8,128)(2,1)S(1)} %get-tuple-element.388), channel_id=1, source_target_pairs={{0,32},{32,64},{64,96},{96,128},{128,160},{160,192},{192,224},{1,3... | collective-permute-start | bytes 1572872 | tf_op jit(solution)/shard_map/while/body/eval_jaxpr/ppermute | solution.py:24
  76.6 12.3 %collective-permute-start.1 = (bf16[2,128,1024]{2,1,0:T(8,128)(2,1)S(1)}, bf16[2,128,1024]{2,1,0:T(8,128)(2,1)S(1)}, u32[]{:S(2)}, u32[]{:S(2)}) collective-permute-start(bf16[2,128,1024]{2,1,0:T(8,128)(2,1)S(1)} %bitcast.107), channel_id=1, source_target_pairs={{0,1},{1,2},{2,3},{3,4},{4,5},{5,6},{6,7},{7,8},{8,9},{9,10},{10,1... | collective-permute-start | bytes 1572872 | tf_op jit(solution)/shard_map/while/body/eval_jaxpr/ppermute | solution.py:13
  76.7 12.2 %collective-permute-start = (bf16[2,128,1024]{2,1,0:T(8,128)(2,1)S(1)}, bf16[2,128,1024]{2,1,0:T(8,128)(2,1)S(1)}, u32[]{:S(2)}, u32[]{:S(2)}) collective-permute-start(bf16[2,128,1024]{2,1,0:T(8,128)(2,1)S(1)} %bitcast.108), channel_id=1, source_target_pairs={{1,0},{2,1},{3,2},{4,3},{5,4},{6,5},{7,6},{8,7},{9,8},{10,9},{11,1... | collective-permute-start | bytes 1572872 | tf_op jit(solution)/shard_map/while/body/eval_jaxpr/ppermute | solution.py:16
  93.8 14.3 %collective-permute-start.2 = (bf16[256,1024]{1,0:T(8,128)(2,1)S(1)}, bf16[256,1024]{1,0:T(8,128)(2,1)S(1)}, u32[]{:S(2)}, u32[]{:S(2)}) collective-permute-start(bf16[256,1024]{1,0:T(8,128)(2,1)S(1)} %get-tuple-element.388), channel_id=1, source_target_pairs={{0,32},{32,64},{64,96},{96,128},{128,160},{160,192},{192,224},{1,3... | collective-permute-start | bytes 1572872 | tf_op jit(solution)/shard_map/while/body/eval_jaxpr/ppermute | solution.py:24
  110.5 12.3 %collective-permute-start.1 = (bf16[2,128,1024]{2,1,0:T(8,128)(2,1)S(1)}, bf16[2,128,1024]{2,1,0:T(8,128)(2,1)S(1)}, u32[]{:S(2)}, u32[]{:S(2)}) collective-permute-start(bf16[2,128,1024]{2,1,0:T(8,128)(2,1)S(1)} %bitcast.107), channel_id=1, source_target_pairs={{0,1},{1,2},{2,3},{3,4},{4,5},{5,6},{6,7},{7,8},{8,9},{9,10},{10,1... | collective-permute-start | bytes 1572872 | tf_op jit(solution)/shard_map/while/body/eval_jaxpr/ppermute | solution.py:13
  110.6 12.2 %collective-permute-start = (bf16[2,128,1024]{2,1,0:T(8,128)(2,1)S(1)}, bf16[2,128,1024]{2,1,0:T(8,128)(2,1)S(1)}, u32[]{:S(2)}, u32[]{:S(2)}) collective-permute-start(bf16[2,128,1024]{2,1,0:T(8,128)(2,1)S(1)} %bitcast.108), channel_id=1, source_target_pairs={{1,0},{2,1},{3,2},{4,3},{5,4},{6,5},{7,6},{8,7},{9,8},{10,9},{11,1... | collective-permute-start | bytes 1572872 | tf_op jit(solution)/shard_map/while/body/eval_jaxpr/ppermute | solution.py:16
  141.2 12.3 %collective-permute-start.1 = (bf16[2,128,1024]{2,1,0:T(8,128)(2,1)S(1)}, bf16[2,128,1024]{2,1,0:T(8,128)(2,1)S(1)}, u32[]{:S(2)}, u32[]{:S(2)}) collective-permute-start(bf16[2,128,1024]{2,1,0:T(8,128)(2,1)S(1)} %bitcast.107), channel_id=1, source_target_pairs={{0,1},{1,2},{2,3},{3,4},{4,5},{5,6},{6,7},{7,8},{8,9},{9,10},{10,1... | collective-permute-start | bytes 1572872 | tf_op jit(solution)/shard_map/while/body/eval_jaxpr/ppermute | solution.py:13
  141.3 12.2 %collective-permute-start = (bf16[2,128,1024]{2,1,0:T(8,128)(2,1)S(1)}, bf16[2,128,1024]{2,1,0:T(8,128)(2,1)S(1)}, u32[]{:S(2)}, u32[]{:S(2)}) collective-permute-start(bf16[2,128,1024]{2,1,0:T(8,128)(2,1)S(1)} %bitcast.108), channel_id=1, source_target_pairs={{1,0},{2,1},{3,2},{4,3},{5,4},{6,5},{7,6},{8,7},{9,8},{10,9},{11,1... | collective-permute-start | bytes 1572872 | tf_op jit(solution)/shard_map/while/body/eval_jaxpr/ppermute | solution.py:16
  171.8 12.3 %collective-permute-start.1 = (bf16[2,128,1024]{2,1,0:T(8,128)(2,1)S(1)}, bf16[2,128,1024]{2,1,0:T(8,128)(2,1)S(1)}, u32[]{:S(2)}, u32[]{:S(2)}) collective-permute-start(bf16[2,128,1024]{2,1,0:T(8,128)(2,1)S(1)} %bitcast.107), channel_id=1, source_target_pairs={{0,1},{1,2},{2,3},{3,4},{4,5},{5,6},{6,7},{7,8},{8,9},{9,10},{10,1... | collective-permute-start | bytes 1572872 | tf_op jit(solution)/shard_map/while/body/eval_jaxpr/ppermute | solution.py:13
  171.9 12.2 %collective-permute-start = (bf16[2,128,1024]{2,1,0:T(8,128)(2,1)S(1)}, bf16[2,128,1024]{2,1,0:T(8,128)(2,1)S(1)}, u32[]{:S(2)}, u32[]{:S(2)}) collective-permute-start(bf16[2,128,1024]{2,1,0:T(8,128)(2,1)S(1)} %bitcast.108), channel_id=1, source_target_pairs={{1,0},{2,1},{3,2},{4,3},{5,4},{6,5},{7,6},{8,7},{9,8},{10,9},{11,1... | collective-permute-start | bytes 1572872 | tf_op jit(solution)/shard_map/while/body/eval_jaxpr/ppermute | solution.py:16
  202.4 12.3 %collective-permute-start.1 = (bf16[2,128,1024]{2,1,0:T(8,128)(2,1)S(1)}, bf16[2,128,1024]{2,1,0:T(8,128)(2,1)S(1)}, u32[]{:S(2)}, u32[]{:S(2)}) collective-permute-start(bf16[2,128,1024]{2,1,0:T(8,128)(2,1)S(1)} %bitcast.107), channel_id=1, source_target_pairs={{0,1},{1,2},{2,3},{3,4},{4,5},{5,6},{6,7},{7,8},{8,9},{9,10},{10,1... | collective-permute-start | bytes 1572872 | tf_op jit(solution)/shard_map/while/body/eval_jaxpr/ppermute | solution.py:13
  202.5 12.3 %collective-permute-start = (bf16[2,128,1024]{2,1,0:T(8,128)(2,1)S(1)}, bf16[2,128,1024]{2,1,0:T(8,128)(2,1)S(1)}, u32[]{:S(2)}, u32[]{:S(2)}) collective-permute-start(bf16[2,128,1024]{2,1,0:T(8,128)(2,1)S(1)} %bitcast.108), channel_id=1, source_target_pairs={{1,0},{2,1},{3,2},{4,3},{5,4},{6,5},{7,6},{8,7},{9,8},{10,9},{11,1... | collective-permute-start | bytes 1572872 | tf_op jit(solution)/shard_map/while/body/eval_jaxpr/ppermute | solution.py:16
  233.0 12.3 %collective-permute-start.1 = (bf16[2,128,1024]{2,1,0:T(8,128)(2,1)S(1)}, bf16[2,128,1024]{2,1,0:T(8,128)(2,1)S(1)}, u32[]{:S(2)}, u32[]{:S(2)}) collective-permute-start(bf16[2,128,1024]{2,1,0:T(8,128)(2,1)S(1)} %bitcast.107), channel_id=1, source_target_pairs={{0,1},{1,2},{2,3},{3,4},{4,5},{5,6},{6,7},{7,8},{8,9},{9,10},{10,1... | collective-permute-start | bytes 1572872 | tf_op jit(solution)/shard_map/while/body/eval_jaxpr/ppermute | solution.py:13
  233.1 12.3 %collective-permute-start = (bf16[2,128,1024]{2,1,0:T(8,128)(2,1)S(1)}, bf16[2,128,1024]{2,1,0:T(8,128)(2,1)S(1)}, u32[]{:S(2)}, u32[]{:S(2)}) collective-permute-start(bf16[2,128,1024]{2,1,0:T(8,128)(2,1)S(1)} %bitcast.108), channel_id=1, source_target_pairs={{1,0},{2,1},{3,2},{4,3},{5,4},{6,5},{7,6},{8,7},{9,8},{10,9},{11,1... | collective-permute-start | bytes 1572872 | tf_op jit(solution)/shard_map/while/body/eval_jaxpr/ppermute | solution.py:16
  263.6 12.3 %collective-permute-start.1 = (bf16[2,128,1024]{2,1,0:T(8,128)(2,1)S(1)}, bf16[2,128,1024]{2,1,0:T(8,128)(2,1)S(1)}, u32[]{:S(2)}, u32[]{:S(2)}) collective-permute-start(bf16[2,128,1024]{2,1,0:T(8,128)(2,1)S(1)} %bitcast.107), channel_id=1, source_target_pairs={{0,1},{1,2},{2,3},{3,4},{4,5},{5,6},{6,7},{7,8},{8,9},{9,10},{10,1... | collective-permute-start | bytes 1572872 | tf_op jit(solution)/shard_map/while/body/eval_jaxpr/ppermute | solution.py:13
  263.6 12.3 %collective-permute-start = (bf16[2,128,1024]{2,1,0:T(8,128)(2,1)S(1)}, bf16[2,128,1024]{2,1,0:T(8,128)(2,1)S(1)}, u32[]{:S(2)}, u32[]{:S(2)}) collective-permute-start(bf16[2,128,1024]{2,1,0:T(8,128)(2,1)S(1)} %bitcast.108), channel_id=1, source_target_pairs={{1,0},{2,1},{3,2},{4,3},{5,4},{6,5},{7,6},{8,7},{9,8},{10,9},{11,1... | collective-permute-start | bytes 1572872 | tf_op jit(solution)/shard_map/while/body/eval_jaxpr/ppermute | solution.py:16
  294.1 12.3 %collective-permute-start.1 = (bf16[2,128,1024]{2,1,0:T(8,128)(2,1)S(1)}, bf16[2,128,1024]{2,1,0:T(8,128)(2,1)S(1)}, u32[]{:S(2)}, u32[]{:S(2)}) collective-permute-start(bf16[2,128,1024]{2,1,0:T(8,128)(2,1)S(1)} %bitcast.107), channel_id=1, source_target_pairs={{0,1},{1,2},{2,3},{3,4},{4,5},{5,6},{6,7},{7,8},{8,9},{9,10},{10,1... | collective-permute-start | bytes 1572872 | tf_op jit(solution)/shard_map/while/body/eval_jaxpr/ppermute | solution.py:13
  294.2 12.3 %collective-permute-start = (bf16[2,128,1024]{2,1,0:T(8,128)(2,1)S(1)}, bf16[2,128,1024]{2,1,0:T(8,128)(2,1)S(1)}, u32[]{:S(2)}, u32[]{:S(2)}) collective-permute-start(bf16[2,128,1024]{2,1,0:T(8,128)(2,1)S(1)} %bitcast.108), channel_id=1, source_target_pairs={{1,0},{2,1},{3,2},{4,3},{5,4},{6,5},{7,6},{8,7},{9,8},{10,9},{11,1... | collective-permute-start | bytes 1572872 | tf_op jit(solution)/shard_map/while/body/eval_jaxpr/ppermute | solution.py:16
  324.7 12.3 %collective-permute-start.1 = (bf16[2,128,1024]{2,1,0:T(8,128)(2,1)S(1)}, bf16[2,128,1024]{2,1,0:T(8,128)(2,1)S(1)}, u32[]{:S(2)}, u32[]{:S(2)}) collective-permute-start(bf16[2,128,1024]{2,1,0:T(8,128)(2,1)S(1)} %bitcast.107), channel_id=1, source_target_pairs={{0,1},{1,2},{2,3},{3,4},{4,5},{5,6},{6,7},{7,8},{8,9},{9,10},{10,1... | collective-permute-start | bytes 1572872 | tf_op jit(solution)/shard_map/while/body/eval_jaxpr/ppermute | solution.py:13
  324.8 12.3 %collective-permute-start = (bf16[2,128,1024]{2,1,0:T(8,128)(2,1)S(1)}, bf16[2,128,1024]{2,1,0:T(8,128)(2,1)S(1)}, u32[]{:S(2)}, u32[]{:S(2)}) collective-permute-start(bf16[2,128,1024]{2,1,0:T(8,128)(2,1)S(1)} %bitcast.108), channel_id=1, source_target_pairs={{1,0},{2,1},{3,2},{4,3},{5,4},{6,5},{7,6},{8,7},{9,8},{10,9},{11,1... | collective-permute-start | bytes 1572872 | tf_op jit(solution)/shard_map/while/body/eval_jaxpr/ppermute | solution.py:16
  (10 other events, 99.3 us)
where the time goes:
time: 356 us; the launch traced here: 353 us
  starting transfers between devices  118 us (33%)
  waiting for transfers between devices  71.4 us (20%)
  loops' own time  47.9 us (13%)
  local copies, waits for them, and re-layouts  41.7 us (12%)
  other arithmetic  37.9 us (11%)
  matrix products  35.7 us (10%)
    ppermute x11, waiting for transfers between devices, from_behind(): lax.ppermute(value, axis, [(source, source + steps) for source in range(f...  67.1 us
    ppermute x11, starting transfers between devices, from_behind(): lax.ppermute(value, axis, [(source, source + steps) for source in range(f...  59.3 us
    ppermute x11, starting transfers between devices, with_halo(): lax.ppermute(lax.slice_in_dim(block, 0, width, axis=dim), axis, backward)  55.7 us
    another operation x1, loops' own time, on_device(): final, unused = lax.scan(turn, start, steps_all)  47.9 us
    dot_general x11, matrix products, part_layer(): z = jnp.dot(agg, weight, preferred_element_type=jnp.float32)  29.3 us
    select_n x11, other arithmetic, turn(): stored = jnp.where(valid, updated, stored)  23 us
    slice x11, local copies, waits for them, and re-layouts, turn(): left_ids = lax.dynamic_index_in_dim(table, before, 0, keepdims=False)[0]  14.2 us
    select_n x11, other arithmetic, turn(): current = jnp.where(section == 0, fresh, incoming)  12.5 us
  transfers between devices with their start and end apart: 33, of which 12 were waited for; matrix products, arithmetic and copies ran while one was open for 11% of the time, Pallas kernels for 0%

commit v1 on v0

v1 whole, which is shorter than its diff:
```python
import functools

import jax
import jax.numpy as jnp
from jax import lax
from jax.experimental import pallas as pl
from jax.experimental.pallas import tpu as pltpu
from jax.sharding import PartitionSpec as P

MESH = pl.DeviceIdType.MESH
CHUNKS = 4


def kernel(
    sections,
    partitions,
    ids_ref,
    coords_ref,
    gain_ref,
    features_ref,
    weight_hbm,
    tiles_hbm,
    out_hbm,
    own,
    halo,
    fwd_stage,
    halo_stage,
    result,
    weight,
    tiles,
    table,
    z_acc,
    own_send,
    own_recv,
    fwd_send,
    halo_send,
    halo_recv,
    feature_sem,
    out_sem,
    load_sem,
):
    p = lax.axis_index("pipe")
    g = lax.axis_index("graph")
    right = lax.rem(g + 1, partitions)
    left = lax.rem(g + partitions - 1, partitions)
    micro_count, chunks, rows, cols = own.shape
    edge = halo.shape[3]
    tile_count = tiles.shape[1]
    slots = rows // edge + 2
    even = lax.rem(p, 2) == 0
    odd = jnp.logical_not(even)
    first = p == 0
    has_next = p < sections - 1
    ahead = jnp.minimum(p + 1, sections - 1)
    behind = jnp.maximum(p - 1, 0)

    load_weight = pltpu.make_async_copy(weight_hbm, weight, load_sem.at[0])
    load_tiles = pltpu.make_async_copy(tiles_hbm, tiles, load_sem.at[1])

    def load_features(m, c):
        return pltpu.make_async_copy(
            features_ref.at[m, :, pl.ds(c * cols, cols)], own.at[m, c], feature_sem.at[m, c]
        )

    def send_own(m, c):
        return pltpu.make_async_remote_copy(
            src_ref=result.at[m, c],
            dst_ref=own.at[m, c],
            send_sem=own_send.at[m, c],
            recv_sem=own_recv.at[m, c],
            device_id=(ahead, g),
            device_id_type=MESH,
        )

    def send_forward(m, side, c):
        return pltpu.make_async_remote_copy(
            src_ref=fwd_stage.at[m, side, c],
            dst_ref=halo.at[m, side, c],
            send_sem=fwd_send.at[m, side, c],
            recv_sem=halo_recv.at[m, side, c],
            device_id=(p, left if side else right),
            device_id_type=MESH,
        )

    def send_halo(m, side, c):
        return pltpu.make_async_remote_copy(
            src_ref=halo_stage.at[m, side, c],
            dst_ref=halo.at[m, side, c],
            send_sem=halo_send.at[m, side, c],
            recv_sem=halo_recv.at[m, side, c],
            device_id=(ahead, left if side else right),
            device_id_type=MESH,
        )

    def save(m, c):
        return pltpu.make_async_copy(
            result.at[m, c], out_hbm.at[m, :, pl.ds(c * cols, cols)], out_sem.at[m, c]
        )

    load_tiles.start()
    load_weight.start()

    @pl.when(first)
    def _():
        for m in range(micro_count):
            for c in range(chunks):
                load_features(m, c).start()

    barrier = pltpu.get_barrier_semaphore()

    def greet(*where):
        for device in where:
            pl.semaphore_signal(barrier, inc=1, device_id=device, device_id_type=MESH)

    @pl.when(even)
    def _():
        greet((p, right), (p, left), (ahead, g), (ahead, right), (ahead, left))

    @pl.when(odd)
    def _():
        greet((behind, g), (behind, right), (behind, left))

    @pl.when(jnp.logical_and(even, p > 0))
    def _():
        greet((behind, g))

    @pl.when(jnp.logical_and(odd, has_next))
    def _():
        greet((ahead, g))

    @pl.when(first)
    def _():
        pl.semaphore_wait(barrier, 5)

    @pl.when(jnp.logical_and(even, p > 0))
    def _():
        pl.semaphore_wait(barrier, 6)

    @pl.when(jnp.logical_and(odd, has_next))
    def _():
        pl.semaphore_wait(barrier, 4)

    @pl.when(p == sections - 1)
    def _():
        pl.semaphore_wait(barrier, 3)

    def picked(block, m, side):
        chosen = ids_ref[m, g, side, 0]
        return jnp.where(chosen == 0, block[:edge], block[edge:])

    def forward(m):
        for c in range(chunks):

            @pl.when(first)
            def _():
                load_features(m, c).wait()

            @pl.when(p > 0)
            def _():
                send_own(m, c).wait_recv()

            block = own[m, c]
            for side in range(2):
                fwd_stage[m, side, c] = picked(block, m, side)
                send_forward(m, side, c).start()

    @pl.when(first)
    def _():
        forward(0)

    load_tiles.wait()

    def build_table(m, carry):
        for d in range(rows // edge):
            for s in range(slots):
                total = jnp.zeros((edge, edge), jnp.float32)
                for t in range(tile_count):
                    here = jnp.logical_and(coords_ref[m, t, 0] == d, coords_ref[m, t, 1] == s)
                    total += tiles[m, t].astype(jnp.float32) * jnp.where(here, 1.0, 0.0)
                table[m, pl.ds(d * edge, edge), pl.ds(s * edge, edge)] = total.astype(jnp.bfloat16)
        return carry

    lax.fori_loop(0, micro_count, build_table, 0)
    load_weight.wait()

    def micro_step(m, carry):
        @pl.when(jnp.logical_and(even, jnp.logical_or(p > 0, m > 0)))
        def _():
            forward(m)

        for c in range(chunks):

            @pl.when(odd)
            def _():
                send_own(m, c).wait_recv()

            agg = jnp.dot(
                table[m, :, :rows], own[m, c], preferred_element_type=jnp.float32
            )
            for side in range(2):
                send_forward(m, side, c).wait_recv()
                agg += jnp.dot(
                    table[m, :, pl.ds(rows + side * edge, edge)],
                    halo[m, side, c],
                    preferred_element_type=jnp.float32,
                )
            part = jnp.dot(
                agg.astype(jnp.bfloat16),
                weight[pl.ds(c * cols, cols), :],
                preferred_element_type=jnp.float32,
            )
            if c == 0:
                z_acc[...] = part
            elif c < chunks - 1:
                z_acc[...] += part
            else:
                act = jnp.maximum(z_acc[...] + part, 0.0)
        scale = 1.0 / jnp.sqrt(jnp.mean(act * act, axis=-1, keepdims=True) + 1e-06)
        for c in range(chunks):
            block = act[:, c * cols : (c + 1) * cols] * scale
            block = (block * gain_ref[:, pl.ds(c * cols, cols)]).astype(jnp.bfloat16)
            result[m, c] = block

            @pl.when(even)
            def _():
                for side in range(2):
                    halo_stage[m, side, c] = picked(block, m, side)
                    send_halo(m, side, c).start()

            @pl.when(has_next)
            def _():
                send_own(m, c).start()

            save(m, c).start()
        return carry

    lax.fori_loop(0, micro_count, micro_step, 0)

    def finish(m, carry):
        for c in range(chunks):
            save(m, c).wait()

            @pl.when(has_next)
            def _():
                send_own(m, c).wait_send()

            @pl.when(even)
            def _():
                for side in range(2):
                    send_forward(m, side, c).wait_send()
                    send_halo(m, side, c).wait_send()

        return carry

    lax.fori_loop(0, micro_count, finish, 0)


def on_device(features, weights, gains, tiles, tile_coords, send_ids):
    micro_count, rows, width = features.shape
    tile_count, edge = tiles.shape[1], tiles.shape[-1]
    slots = rows // edge + 2
    cols = width // CHUNKS
    per_chunk = (micro_count, CHUNKS)
    per_side = (micro_count, 2, CHUNKS)
    result = pl.pallas_call(
        functools.partial(kernel, lax.axis_size("pipe"), lax.axis_size("graph")),
        out_shape=jax.ShapeDtypeStruct((micro_count, rows, width), jnp.bfloat16),
        in_specs=[
            pl.BlockSpec(memory_space=pltpu.SMEM),
            pl.BlockSpec(memory_space=pltpu.SMEM),
            pl.BlockSpec(memory_space=pltpu.VMEM),
            pl.BlockSpec(memory_space=pl.ANY),
            pl.BlockSpec(memory_space=pl.ANY),
            pl.BlockSpec(memory_space=pl.ANY),
        ],
        out_specs=pl.BlockSpec(memory_space=pl.ANY),
        scratch_shapes=[
            pltpu.VMEM(per_chunk + (rows, cols), jnp.bfloat16),
            pltpu.VMEM(per_side + (edge, cols), jnp.bfloat16),
            pltpu.VMEM(per_side + (edge, cols), jnp.bfloat16),
            pltpu.VMEM(per_side + (edge, cols), jnp.bfloat16),
            pltpu.VMEM(per_chunk + (rows, cols), jnp.bfloat16),
            pltpu.VMEM((width, width), jnp.bfloat16),
            pltpu.VMEM((micro_count, tile_count, edge, edge), jnp.bfloat16),
            pltpu.VMEM((micro_count, rows, slots * edge), jnp.bfloat16),
            pltpu.VMEM((rows, width), jnp.float32),
            pltpu.SemaphoreType.DMA(per_chunk),
            pltpu.SemaphoreType.DMA(per_chunk),
            pltpu.SemaphoreType.DMA(per_side),
            pltpu.SemaphoreType.DMA(per_side),
            pltpu.SemaphoreType.DMA(per_side),
            pltpu.SemaphoreType.DMA(per_chunk),
            pltpu.SemaphoreType.DMA(per_chunk),
            pltpu.SemaphoreType.DMA((2,)),
        ],
        compiler_params=pltpu.CompilerParams(
            collective_id=0, has_side_effects=True, vmem_limit_bytes=48 * 1024 * 1024
        ),
    )(send_ids, tile_coords, gains, features, weights[0], tiles)
    return result[None]


def solution(mesh):
    placed = (
        P(None, "graph", None),
        P("pipe", None, None),
        P("pipe", None),
        P(None, "graph", None, None),
        P(None, "graph", None),
        P(),
    )
    return jax.shard_map(
        on_device,
        mesh=mesh,
        in_specs=placed,
        out_specs=P("pipe", None, "graph", None),
        check_vma=False,
    )
```

time: 356 us -> 126 us (0.35)
  the two profiles are of different devices: /device:TPU:1 before, /device:TPU:7 now
where the time goes in v1:
time: 126 us
  Pallas kernels  120 us (95%)
  local copies, waits for them, and re-layouts  6.62 us (5%)
    pallas_call x1, Pallas kernels, on_device(): pl.pallas_call(functools.partial(kernel, lax.axis_size('pipe'), lax.axis_...  120 us
    unnamed x9, local copies, waits for them, and re-layouts  6.62 us

profile of v1, /device:TPU:7, one launch (start us, length us, event | category | flops | bytes accessed | tf_op | source)
XLA Modules:
  0.0 126.2 jit_solution(3292403298905675984)
XLA Ops:
  0.0 0.8 copy.8.coords_ref
  0.8 0.8 copy.7.ids_ref
  1.6 0.0 copy-start
  1.6 1.6 %copy-done = bf16[4,256,1024]{2,1,0:T(8,128)(2,1)S(1)} copy-done((bf16[4,256,1024]{2,1,0:T(8,128)(2,1)S(1)}, bf16[4,256,1024]{2,1,0:T(8,128)(2,1)}, u32[]{:S(2)}) %copy-start) | copy-done | bytes 2097176
  3.2 0.0 copy-start.1
  3.2 1.4 %copy-done.1 = bf16[4,12,128,128]{3,2,1,0:T(8,128)(2,1)S(1)} copy-done((bf16[4,12,128,128]{3,2,1,0:T(8,128)(2,1)S(1)}, bf16[4,12,128,128]{3,2,1,0:T(8,128)(2,1)}, u32[]{:S(2)}) %copy-start.1) | copy-done | bytes 1572888
  4.6 0.0 copy-start.2
  4.6 0.7 copy-done.2
  5.3 119.6 %shard_map.64 = bf16[4,256,1024]{2,1,0:T(8,128)(2,1)S(1)} custom-call(s32[4,32,2,1]{3,2,1,0:T(2,128)S(1)} %copy.7.ids_ref, s32[4,12,2]{2,1,0:T(8,128)S(1)} %copy.8.coords_ref, f32[1,1024]{1,0:T(1,128)S(1)} %copy-done.2, bf16[4,256,1024]{2,1,0:T(8,128)(2,1)S(1)} %copy-done, bf16[1024,1024]{1,0:T(8,128)(2,1)} %bitcast.3, bf16[4,12,128,128]{3,2,1,0:T(8,128)(2,1)S(1)} %copy-done.1), custom_call_target="tpu_custom_call" | custom-call | tf_op jit(solution)/shard_map/pallas_call | solution.py:265
  124.9 1.3 %copy.10 = bf16[1,4,256,1024]{3,2,1,0:T(8,128)(2,1)} copy(bf16[1,4,256,1024]{3,2,1,0:T(8,128)(2,1)S(1)} %bitcast.2) | data formatting | bytes 4194304
Async XLA Ops:
  1.6 1.6 %copy-start = (bf16[4,256,1024]{2,1,0:T(8,128)(2,1)S(1)}, bf16[4,256,1024]{2,1,0:T(8,128)(2,1)}, u32[]{:S(2)}) copy-start(bf16[4,256,1024]{2,1,0:T(8,128)(2,1)} %features_ref.1) | copy-start | bytes 6291460
  3.2 1.4 %copy-start.1 = (bf16[4,12,128,128]{3,2,1,0:T(8,128)(2,1)S(1)}, bf16[4,12,128,128]{3,2,1,0:T(8,128)(2,1)}, u32[]{:S(2)}) copy-start(bf16[4,12,128,128]{3,2,1,0:T(8,128)(2,1)} %tiles_hbm.1) | copy-start | bytes 4718596
  4.6 0.7 copy-start.2

commit v2 on v1

--- a/solution.py
+++ b/solution.py
@@ -16,7 +16,7 @@
     partitions,
     ids_ref,
     coords_ref,
-    gain_ref,
+    gain_hbm,
     features_ref,
     weight_hbm,
     tiles_hbm,
@@ -27,6 +27,7 @@
     halo_stage,
     result,
     weight,
+    gain_ref,
     tiles,
     table,
     z_acc,
@@ -55,6 +56,7 @@
     behind = jnp.maximum(p - 1, 0)
 
     load_weight = pltpu.make_async_copy(weight_hbm, weight, load_sem.at[0])
+    load_gain = pltpu.make_async_copy(gain_hbm, gain_ref, load_sem.at[2])
     load_tiles = pltpu.make_async_copy(tiles_hbm, tiles, load_sem.at[1])
 
     def load_features(m, c):
@@ -99,6 +101,7 @@
 
     load_tiles.start()
     load_weight.start()
+    load_gain.start()
 
     @pl.when(first)
     def _():
@@ -145,11 +148,11 @@
         pl.semaphore_wait(barrier, 3)
 
     def picked(block, m, side):
-        chosen = ids_ref[m, g, side, 0]
+        chosen = ids_ref[m, side, 0, g]
         return jnp.where(chosen == 0, block[:edge], block[edge:])
 
-    def forward(m):
-        for c in range(chunks):
+    def forward(m, pieces=range(chunks)):
+        for c in pieces:
 
             @pl.when(first)
             def _():
@@ -175,18 +178,23 @@
             for s in range(slots):
                 total = jnp.zeros((edge, edge), jnp.float32)
                 for t in range(tile_count):
-                    here = jnp.logical_and(coords_ref[m, t, 0] == d, coords_ref[m, t, 1] == s)
+                    here = jnp.logical_and(coords_ref[m, 0, t] == d, coords_ref[m, 1, t] == s)
                     total += tiles[m, t].astype(jnp.float32) * jnp.where(here, 1.0, 0.0)
                 table[m, pl.ds(d * edge, edge), pl.ds(s * edge, edge)] = total.astype(jnp.bfloat16)
         return carry
 
     lax.fori_loop(0, micro_count, build_table, 0)
     load_weight.wait()
+    load_gain.wait()
+
+    @pl.when(jnp.logical_and(even, p > 0))
+    def _():
+        forward(0)
 
     def micro_step(m, carry):
-        @pl.when(jnp.logical_and(even, jnp.logical_or(p > 0, m > 0)))
+        @pl.when(jnp.logical_and(even, m < micro_count - 1))
         def _():
-            forward(m)
+            forward(m + 1, range(chunks - 1))
 
         for c in range(chunks):
 
@@ -220,17 +228,25 @@
             block = act[:, c * cols : (c + 1) * cols] * scale
             block = (block * gain_ref[:, pl.ds(c * cols, cols)]).astype(jnp.bfloat16)
             result[m, c] = block
-
-            @pl.when(even)
-            def _():
+            for side in range(2):
+                halo_stage[m, side, c] = picked(block, m, side)
+
+        @pl.when(jnp.logical_and(even, m < micro_count - 1))
+        def _():
+            forward(m + 1, range(chunks - 1, chunks))
+
+        @pl.when(even)
+        def _():
+            for c in range(chunks):
                 for side in range(2):
-                    halo_stage[m, side, c] = picked(block, m, side)
                     send_halo(m, side, c).start()
 
-            @pl.when(has_next)
-            def _():
+        @pl.when(has_next)
+        def _():
+            for c in range(chunks):
                 send_own(m, c).start()
 
+        for c in range(chunks):
             save(m, c).start()
         return carry
 
@@ -268,10 +284,10 @@
         in_specs=[
             pl.BlockSpec(memory_space=pltpu.SMEM),
             pl.BlockSpec(memory_space=pltpu.SMEM),
-            pl.BlockSpec(memory_space=pltpu.VMEM),
-            pl.BlockSpec(memory_space=pl.ANY),
-            pl.BlockSpec(memory_space=pl.ANY),
-            pl.BlockSpec(memory_space=pl.ANY),
+            pl.BlockSpec(memory_space=pltpu.HBM),
+            pl.BlockSpec(memory_space=pltpu.HBM),
+            pl.BlockSpec(memory_space=pltpu.HBM),
+            pl.BlockSpec(memory_space=pltpu.HBM),
         ],
         out_specs=pl.BlockSpec(memory_space=pl.ANY),
         scratch_shapes=[
@@ -281,6 +297,7 @@
             pltpu.VMEM(per_side + (edge, cols), jnp.bfloat16),
             pltpu.VMEM(per_chunk + (rows, cols), jnp.bfloat16),
             pltpu.VMEM((width, width), jnp.bfloat16),
+            pltpu.VMEM((1, width), jnp.float32),
             pltpu.VMEM((micro_count, tile_count, edge, edge), jnp.bfloat16),
             pltpu.VMEM((micro_count, rows, slots * edge), jnp.bfloat16),
             pltpu.VMEM((rows, width), jnp.float32),
@@ -291,12 +308,19 @@
             pltpu.SemaphoreType.DMA(per_side),
             pltpu.SemaphoreType.DMA(per_chunk),
             pltpu.SemaphoreType.DMA(per_chunk),
-            pltpu.SemaphoreType.DMA((2,)),
+            pltpu.SemaphoreType.DMA((3,)),
         ],
         compiler_params=pltpu.CompilerParams(
-            collective_id=0, has_side_effects=True, vmem_limit_bytes=48 * 1024 * 1024
+            collective_id=0, has_side_effects=True, vmem_limit_bytes=60 * 1024 * 1024
         ),
-    )(send_ids, tile_coords, gains, features, weights[0], tiles)
+    )(
+        jnp.transpose(send_ids, (0, 2, 3, 1)),
+        jnp.transpose(tile_coords, (0, 2, 1)),
+        gains,
+        features,
+        weights[0],
+        tiles,
+    )
     return result[None]
 
 

time: 126 us -> 114 us (0.905)
  Pallas kernels: 120 us -> 111 us
  local copies, waits for them, and re-layouts: 6.62 us -> 3.08 us
    pallas_call x1, Pallas kernels: 120 us -> 111 us  [on_device(): pl.pallas_call(functools.partial(kernel, lax.axis_size('pipe'), lax.axis_...]
    unnamed x9 -> x1, local copies, waits for them, and re-layouts: 6.62 us -> 3.08 us
where the time goes in v2:
time: 114 us
  Pallas kernels  111 us (97%)
  local copies, waits for them, and re-layouts  3.08 us (3%)
    pallas_call x1, Pallas kernels, on_device(): pl.pallas_call(functools.partial(kernel, lax.axis_size('pipe'), lax.axis_...  111 us
    unnamed x1, local copies, waits for them, and re-layouts  3.08 us

profile of v2, /device:TPU:7, one launch (start us, length us, event | category | flops | bytes accessed | tf_op | source)
XLA Modules:
  0.0 114.0 jit_solution(15969189684216113865)
XLA Ops:
  0.0 110.9 %shard_map.64 = bf16[4,256,1024]{2,1,0:T(8,128)(2,1)} custom-call(s32[4,2,1,32]{3,2,1,0:T(1,128)} %bitcast.6, s32[4,2,12]{2,1,0:T(2,128)} %bitcast.7, f32[1,1024]{1,0:T(1,128)} %gain_hbm.1, bf16[4,256,1024]{2,1,0:T(8,128)(2,1)} %features_ref.1, bf16[1024,1024]{1,0:T(8,128)(2,1)} %bitcast.5, bf16[4,12,128,128]{3,2,1,0:T(8,128)(2,1)} %tiles_hbm.1), custom_call_target="tpu_custom_call" | custom-call | tf_op jit(solution)/shard_map/pallas_call | solution.py:281
  110.9 3.1 %copy.8 = bf16[1,4,256,1024]{3,2,1,0:T(8,128)(2,1)} copy(bf16[1,4,256,1024]{3,2,1,0:T(8,128)(2,1)} %bitcast.4) | data formatting | bytes 4194304

commit v3 on v2

--- a/solution.py
+++ b/solution.py
@@ -202,22 +202,27 @@
             def _():
                 send_own(m, c).wait_recv()
 
-            agg = jnp.dot(
-                table[m, :, :rows], own[m, c], preferred_element_type=jnp.float32
-            )
             for side in range(2):
                 send_forward(m, side, c).wait_recv()
-                agg += jnp.dot(
-                    table[m, :, pl.ds(rows + side * edge, edge)],
-                    halo[m, side, c],
-                    preferred_element_type=jnp.float32,
-                )
-            part = jnp.dot(
-                agg.astype(jnp.bfloat16),
-                weight[pl.ds(c * cols, cols), :],
+            agg = jnp.dot(
+                table[m, :, pl.ds(0, rows)], own[m, c], preferred_element_type=jnp.float32
+            )
+            agg += jnp.dot(
+                table[m, :, pl.ds(rows, 2 * edge)],
+                halo[m, :, c].reshape(2 * edge, cols),
                 preferred_element_type=jnp.float32,
             )
             if c == 0:
+                head = agg.astype(jnp.bfloat16)
+                continue
+            if c == 1:
+                agg = jnp.concatenate([head, agg.astype(jnp.bfloat16)], axis=1)
+            part = jnp.dot(
+                agg.astype(jnp.bfloat16),
+                weight[pl.ds((c + 1) * cols - agg.shape[1], agg.shape[1]), :],
+                preferred_element_type=jnp.float32,
+            )
+            if c == 1:
                 z_acc[...] = part
             elif c < chunks - 1:
                 z_acc[...] += part

time: 114 us -> 112 us (0.982)
  Pallas kernels: 111 us -> 109 us
    pallas_call x1, Pallas kernels: 111 us -> 109 us  [on_device(): pl.pallas_call(functools.partial(kernel, lax.axis_size('pipe'), lax.axis_...]
where the time goes in v3:
time: 112 us
  Pallas kernels  109 us (97%)
  local copies, waits for them, and re-layouts  3.08 us (3%)
    pallas_call x1, Pallas kernels, on_device(): pl.pallas_call(functools.partial(kernel, lax.axis_size('pipe'), lax.axis_...  109 us
    unnamed x1, local copies, waits for them, and re-layouts  3.08 us

profile of v3, /device:TPU:7, one launch (start us, length us, event | category | flops | bytes accessed | tf_op | source)
XLA Modules:
  0.0 111.6 jit_solution(6789004573252612618)
XLA Ops:
  0.0 108.5 %shard_map.64 = bf16[4,256,1024]{2,1,0:T(8,128)(2,1)} custom-call(s32[4,2,1,32]{3,2,1,0:T(1,128)} %bitcast.6, s32[4,2,12]{2,1,0:T(2,128)} %bitcast.7, f32[1,1024]{1,0:T(1,128)} %gain_hbm.1, bf16[4,256,1024]{2,1,0:T(8,128)(2,1)} %features_ref.1, bf16[1024,1024]{1,0:T(8,128)(2,1)} %bitcast.5, bf16[4,12,128,128]{3,2,1,0:T(8,128)(2,1)} %tiles_hbm.1), custom_call_target="tpu_custom_call" | custom-call | tf_op jit(solution)/shard_map/pallas_call | solution.py:286
  108.5 3.1 %copy.8 = bf16[1,4,256,1024]{3,2,1,0:T(8,128)(2,1)} copy(bf16[1,4,256,1024]{3,2,1,0:T(8,128)(2,1)} %bitcast.4) | data formatting | bytes 4194304

commit v4 on v3

--- a/solution.py
+++ b/solution.py
@@ -233,8 +233,6 @@
             block = act[:, c * cols : (c + 1) * cols] * scale
             block = (block * gain_ref[:, pl.ds(c * cols, cols)]).astype(jnp.bfloat16)
             result[m, c] = block
-            for side in range(2):
-                halo_stage[m, side, c] = picked(block, m, side)
 
         @pl.when(jnp.logical_and(even, m < micro_count - 1))
         def _():
@@ -244,6 +242,7 @@
         def _():
             for c in range(chunks):
                 for side in range(2):
+                    halo_stage[m, side, c] = picked(result[m, c], m, side)
                     send_halo(m, side, c).start()
 
         @pl.when(has_next)

time: 112 us -> 111 us (level)
  no operation moved by 1% of the time
where the time goes in v4:
time: 111 us
  Pallas kernels  108 us (97%)
  local copies, waits for them, and re-layouts  3.08 us (3%)
    pallas_call x1, Pallas kernels, on_device(): pl.pallas_call(functools.partial(kernel, lax.axis_size('pipe'), lax.axis_...  108 us
    unnamed x1, local copies, waits for them, and re-layouts  3.08 us

profile of v4, /device:TPU:7, one launch (start us, length us, event | category | flops | bytes accessed | tf_op | source)
XLA Modules:
  0.0 110.9 jit_solution(11987510164007137435)
XLA Ops:
  0.0 107.8 %shard_map.64 = bf16[4,256,1024]{2,1,0:T(8,128)(2,1)} custom-call(s32[4,2,1,32]{3,2,1,0:T(1,128)} %bitcast.6, s32[4,2,12]{2,1,0:T(2,128)} %bitcast.7, f32[1,1024]{1,0:T(1,128)} %gain_hbm.1, bf16[4,256,1024]{2,1,0:T(8,128)(2,1)} %features_ref.1, bf16[1024,1024]{1,0:T(8,128)(2,1)} %bitcast.5, bf16[4,12,128,128]{3,2,1,0:T(8,128)(2,1)} %tiles_hbm.1), custom_call_target="tpu_custom_call" | custom-call | tf_op jit(solution)/shard_map/pallas_call | solution.py:285
  107.8 3.1 %copy.8 = bf16[1,4,256,1024]{3,2,1,0:T(8,128)(2,1)} copy(bf16[1,4,256,1024]{3,2,1,0:T(8,128)(2,1)} %bitcast.4) | data formatting | bytes 4194304
